TPU v7x, 1024 devices: a whole 4x8x16 slice. The times are simulated.
1024 devices in a mesh: grp: 128 (over x, z, core), leaf: 8 (over y).
Axes of the slice: x: 4, y: 8, z: 16, core: 2. Of those that a mesh axis runs over, the one named last changes fastest.
Arguments:
- inputs: float32 [2097152, 64], P(('grp', 'leaf')), may hold values from -6 to 6
- freqs: float32 [64, 256], replicated, may hold values from -0.75 to 0.75
- phases: float32 [256], replicated, may hold values from -3.140625 to 3.140625
- sample_weight: float32 [2097152], P(('grp', 'leaf')), as said below
- stored: float32 [1024, 256, 256], P(('grp', 'leaf')), as said below
- root: int32 [1024], replicated, may hold values from 0 to 1023, each once
Outputs:
- factor: float32 [256, 256], replicated
- basis: float32 [2097152, 256], P(('grp', 'leaf'))
Inputs may be any that keep to these rules, and one draw needn't show every extreme that they name: `root`: each device index once, in the order grp first, leaf second; only the first entry is read. `stored`: each slot is upper triangular with a positive diagonal. `sample_weight`: positive row weights.
All inputs are finite; a program needn't handle non-finite values.
Results may differ from a plain program's by a relative error of at most 0.0003.
Values sent between devices are 32-bit elements; how exact they have to be, the bound alone decides.
A program may use at most 32 MiB of HBM per device.

v0:
```python
import math

import jax
import jax.numpy as jnp
from jax import lax
from jax.sharding import PartitionSpec as P


def partner(array, axis, distance):
    return lax.ppermute(array, axis, [(i, i ^ 1 << distance) for i in range(lax.axis_size(axis))])


def spread(array, axis, root):
    mine = lax.axis_index(axis) == root
    return lax.psum(jnp.where(mine, array, jnp.zeros_like(array)), axis)


def per_device(inputs, freqs, phases, sample_weight, stored, root):
    total_rows = inputs.shape[0] * lax.axis_size("grp") * lax.axis_size("leaf")
    norm_scale = 1.0 / math.sqrt(total_rows)
    proj = jnp.dot(inputs, freqs, precision=lax.Precision.HIGHEST) + phases[None, :]
    features = jnp.sqrt(sample_weight)[:, None] * jnp.cos(proj) * norm_scale
    gram = lax.dot_general(
        features, features, (((0,), (0,)), ((), ())), precision=lax.Precision.HIGHEST
    )
    running = stored[0]
    payload = gram
    for bit_leaf in range(lax.axis_size("leaf").bit_length() - 1):
        payload = payload + partner(payload, "leaf", bit_leaf)
    for bit_grp in range(lax.axis_size("grp").bit_length() - 1):
        payload = payload + partner(payload, "grp", bit_grp)
    gram = payload
    carried = spread(running, ("grp", "leaf"), root[0])
    gram = jnp.dot(carried.T, carried, precision=lax.Precision.HIGHEST) + gram
    lower = jnp.linalg.cholesky(gram)
    solved = jax.scipy.linalg.solve_triangular(lower, features.T, lower=True)
    basis = solved.T * math.sqrt(total_rows)
    return (lower.T, basis)


def solution(mesh):
    return jax.shard_map(
        per_device,
        mesh=mesh,
        in_specs=(
            P(("grp", "leaf"), None),
            P(),
            P(),
            P(("grp", "leaf")),
            P(("grp", "leaf"), None, None),
            P(),
        ),
        out_specs=(P(), P(("grp", "leaf"), None)),
        check_vma=False,
    )
```

profile of v0, /device:TPU:1, one launch (start us, length us, event | category | flops | bytes accessed | tf_op | source)
XLA Modules:
  0.0 718.3 jit_solution(11575255056918623297)
XLA Ops:
  7.2 0.0 copy-start
  7.2 0.0 all-reduce.3.cloned.1.call-start
  7.2 0.8 sqrt.3
  8.0 0.3 copy-done
  8.2 9.5 %fusion.2 = f32[2048,256]{1,0:T(8,128)S(1)} fusion(f32[2048,64]{0,1:T(8,128)S(1)} %copy-done, f32[64,256]{1,0:T(8,128)} %param.7, f32[256]{0:T(256)} %param.8, f32[2048]{0:T(1024)S(1)} %sqrt.3), kind=kOutput, calls=%fused_computation.5 | convolution fusion | flops 404226048 | bytes 2696192 | tf_op jit(solution)/shard_map/dot_general | solution.py:21
  17.8 3.6 fusion.16
  21.4 4.0 collective-permute-start
  25.4 3.7 collective-permute-done
  29.2 6.3 collective-permute-start.1
  35.6 6.7 collective-permute-done.1
  42.3 13.1 %collective-permute-start.2 = (f32[256,256]{0,1:T(8,128)S(1)}, f32[256,256]{0,1:T(8,128)S(1)}, u32[]{:S(2)}, u32[]{:S(2)}) collective-permute-start(f32[256,256]{0,1:T(8,128)S(1)} %add.75), channel_id=1, source_target_pairs={{0,4},{1,5},{2,6},{3,7},{4,0},{5,1},{6,2},{7,3},{8,12},{9,13},{10,... | collective-permute-start | bytes 786440 | tf_op jit(solution)/shard_map/ppermute | solution.py:10
  55.4 6.6 collective-permute-done.2
  62.0 0.0 copy-start.1
  62.0 19.6 %collective-permute-start.3 = (f32[256,256]{0,1:T(8,128)S(1)}, f32[256,256]{0,1:T(8,128)S(1)}, u32[]{:S(2)}, u32[]{:S(2)}) collective-permute-start(f32[256,256]{0,1:T(8,128)S(1)} %add.76), channel_id=1, source_target_pairs={{0,8},{8,0},{16,24},{24,16},{32,40},{40,32},{48,56},{56,48},{64,72... | collective-permute-start | bytes 786440 | tf_op jit(solution)/shard_map/ppermute | solution.py:10
  81.6 1.1 collective-permute-done.3
  82.8 1.9 collective-permute-start.4
  84.7 7.5 %collective-permute-done.4 = f32[256,256]{0,1:T(8,128)S(1)} collective-permute-done((f32[256,256]{0,1:T(8,128)S(1)}, f32[256,256]{0,1:T(8,128)S(1)}, u32[]{:S(2)}, u32[]{:S(2)}) %collective-permute-start.4) | collective-permute-done | bytes 262176 | tf_op jit(solution)/shard_map/ppermute | solution.py:10
  92.2 1.9 collective-permute-start.5
  94.1 14.7 %collective-permute-done.5 = f32[256,256]{0,1:T(8,128)S(1)} collective-permute-done((f32[256,256]{0,1:T(8,128)S(1)}, f32[256,256]{0,1:T(8,128)S(1)}, u32[]{:S(2)}, u32[]{:S(2)}) %collective-permute-start.5) | collective-permute-done | bytes 262176 | tf_op jit(solution)/shard_map/ppermute | solution.py:10
  108.8 1.9 collective-permute-start.6
  110.8 25.1 %collective-permute-done.6 = f32[256,256]{0,1:T(8,128)S(1)} collective-permute-done((f32[256,256]{0,1:T(8,128)S(1)}, f32[256,256]{0,1:T(8,128)S(1)}, u32[]{:S(2)}, u32[]{:S(2)}) %collective-permute-start.6) | collective-permute-done | bytes 262176 | tf_op jit(solution)/shard_map/ppermute | solution.py:10
  135.9 15.4 %collective-permute-start.7 = (f32[256,256]{0,1:T(8,128)S(1)}, f32[256,256]{0,1:T(8,128)S(1)}, u32[]{:S(2)}, u32[]{:S(2)}) collective-permute-start(f32[256,256]{0,1:T(8,128)S(1)} %add.80), channel_id=1, source_target_pairs={{0,128},{8,136},{16,144},{24,152},{32,160},{40,168},{48,176},{56,1... | collective-permute-start | bytes 786440 | tf_op jit(solution)/shard_map/ppermute | solution.py:10
  151.3 14.7 %collective-permute-done.7 = f32[256,256]{0,1:T(8,128)S(1)} collective-permute-done((f32[256,256]{0,1:T(8,128)S(1)}, f32[256,256]{0,1:T(8,128)S(1)}, u32[]{:S(2)}, u32[]{:S(2)}) %collective-permute-start.7) | collective-permute-done | bytes 262176 | tf_op jit(solution)/shard_map/ppermute | solution.py:10
  166.0 3.2 collective-permute-start.8
  169.2 1.2 slice.50
  171.1 0.0 copy-done.1
  171.1 0.7 select_bitcast_fusion
  171.8 0.0 all-reduce.3.cloned.1.call-update
  171.8 3.4 collective-permute-done.8
  175.3 4.7 collective-permute-start.9
  180.0 463.3 %all-reduce.3.cloned.1.call-done = f32[256,256]{1,0:T(8,128)} async-done(((f32[256,256]{1,0:T(8,128)}), f32[256,256]{1,0:T(8,128)}) %all-reduce.3.cloned.1.call-update) | async-done | bytes 262160 | tf_op jit(solution)/shard_map/psum | solution.py:15
  643.3 1.6 fusion.15
  645.0 0.0 collective-permute-done.9
  645.0 0.1 add_add_fusion
  645.0 0.1 copy.11
  645.2 11.7 %cholesky.49 = f32[128,128]{1,0:T(8,128)S(1)} custom-call(f32[128,128]{1,0:T(8,128)S(1)} %cholesky.115), custom_call_target="Cholesky" | custom-call | tf_op jit(solution)/shard_map/jit(cholesky)/cholesky | solution.py:35
  657.0 9.8 %custom-call.15 = f32[1,128,128]{1,2,0:T(8,128)S(1)} custom-call(f32[1,128,128]{2,1,0:T(8,128)S(1)} %get-tuple-element.27), custom_call_target="InvertDiagBlocksLowerTriangular" | custom-call | tf_op jit(solution)/shard_map/jit(cholesky)/cholesky | solution.py:35
  666.8 0.2 constant_dynamic-update-slice_fusion.1
  667.0 0.3 convolution_subtract_fusion.1
  667.3 11.7 %cholesky.103 = f32[128,128]{1,0:T(8,128)S(1)} custom-call(f32[128,128]{1,0:T(8,128)S(1)} %convolution_subtract_fusion.1), custom_call_target="Cholesky" | custom-call | tf_op jit(solution)/shard_map/jit(cholesky)/cholesky | solution.py:35
  679.1 0.6 compare_reduce_fusion
  681.0 0.8 copy.12
  681.9 0.1 triangular_solve.42
  682.0 3.8 while.1
  682.0 0.6 fusion.28
  682.5 1.3 bitcast_dynamic-update-slice_fusion.2
  683.9 0.6 fusion.28
  684.5 1.3 bitcast_dynamic-update-slice_fusion.2
  685.8 19.7 %custom-call.16 = f32[2,128,128]{1,2,0:T(8,128)S(1)} custom-call(f32[2,128,128]{2,1,0:T(8,128)S(1)} %get-tuple-element.9), custom_call_target="InvertDiagBlocksLowerTriangular" | custom-call | tf_op jit(solution)/shard_map/jit(_solve_triangular)/triangular_solve | solution.py:36
  705.5 1.1 fusion.4
  706.5 1.8 convolution_subtract_fusion
  708.4 1.1 fusion.10
  709.4 0.2 fusion.3
  709.6 1.8 copy.13
  (19 shorter events, 0.5 us)
Async XLA Ops:
  7.2 1.1 copy-start
  7.2 636.2 %all-reduce.3.cloned.1.call-start = ((), (), s32[]{:S(2)}) async-start(), calls=%async_computation | async-start | bytes 524288 | tf_op jit(solution)/shard_map/psum | solution.py:15
  21.4 7.8 %collective-permute-start = (f32[256,256]{0,1:T(8,128)S(1)}, f32[256,256]{0,1:T(8,128)S(1)}, u32[]{:S(2)}, u32[]{:S(2)}) collective-permute-start(f32[256,256]{0,1:T(8,128)S(1)} %fusion.16), channel_id=1, source_target_pairs={{0,1},{1,0},{2,3},{3,2},{4,5},{5,4},{6,7},{7,6},{8,9},{9,8},{10,11... | collective-permute-start | bytes 786440 | tf_op jit(solution)/shard_map/ppermute | solution.py:10
  29.2 13.0 %collective-permute-start.1 = (f32[256,256]{0,1:T(8,128)S(1)}, f32[256,256]{0,1:T(8,128)S(1)}, u32[]{:S(2)}, u32[]{:S(2)}) collective-permute-start(f32[256,256]{0,1:T(8,128)S(1)} %add.74), channel_id=1, source_target_pairs={{0,2},{1,3},{2,0},{3,1},{4,6},{5,7},{6,4},{7,5},{8,10},{9,11},{10,... | collective-permute-start | bytes 786440 | tf_op jit(solution)/shard_map/ppermute | solution.py:10
  42.3 19.7 %collective-permute-start.2 = (f32[256,256]{0,1:T(8,128)S(1)}, f32[256,256]{0,1:T(8,128)S(1)}, u32[]{:S(2)}, u32[]{:S(2)}) collective-permute-start(f32[256,256]{0,1:T(8,128)S(1)} %add.75), channel_id=1, source_target_pairs={{0,4},{1,5},{2,6},{3,7},{4,0},{5,1},{6,2},{7,3},{8,12},{9,13},{10,... | collective-permute-start | bytes 786440 | tf_op jit(solution)/shard_map/ppermute | solution.py:10
  62.0 109.1 %copy-start.1 = (f32[1,256,256]{2,1,0:T(8,128)S(1)}, f32[1,256,256]{2,1,0:T(8,128)}, u32[]{:S(2)}) copy-start(f32[1,256,256]{2,1,0:T(8,128)} %param.10) | copy-start | bytes 786436
  62.0 20.8 %collective-permute-start.3 = (f32[256,256]{0,1:T(8,128)S(1)}, f32[256,256]{0,1:T(8,128)S(1)}, u32[]{:S(2)}, u32[]{:S(2)}) collective-permute-start(f32[256,256]{0,1:T(8,128)S(1)} %add.76), channel_id=1, source_target_pairs={{0,8},{8,0},{16,24},{24,16},{32,40},{40,32},{48,56},{56,48},{64,72... | collective-permute-start | bytes 786440 | tf_op jit(solution)/shard_map/ppermute | solution.py:10
  82.8 9.4 %collective-permute-start.4 = (f32[256,256]{0,1:T(8,128)S(1)}, f32[256,256]{0,1:T(8,128)S(1)}, u32[]{:S(2)}, u32[]{:S(2)}) collective-permute-start(f32[256,256]{0,1:T(8,128)S(1)} %add.77), channel_id=1, source_target_pairs={{0,16},{8,24},{16,0},{24,8},{32,48},{40,56},{48,32},{56,40},{64,80... | collective-permute-start | bytes 786440 | tf_op jit(solution)/shard_map/ppermute | solution.py:10
  92.2 16.6 %collective-permute-start.5 = (f32[256,256]{0,1:T(8,128)S(1)}, f32[256,256]{0,1:T(8,128)S(1)}, u32[]{:S(2)}, u32[]{:S(2)}) collective-permute-start(f32[256,256]{0,1:T(8,128)S(1)} %add.78), channel_id=1, source_target_pairs={{0,32},{8,40},{16,48},{24,56},{32,0},{40,8},{48,16},{56,24},{64,96... | collective-permute-start | bytes 786440 | tf_op jit(solution)/shard_map/ppermute | solution.py:10
  108.8 27.0 %collective-permute-start.6 = (f32[256,256]{0,1:T(8,128)S(1)}, f32[256,256]{0,1:T(8,128)S(1)}, u32[]{:S(2)}, u32[]{:S(2)}) collective-permute-start(f32[256,256]{0,1:T(8,128)S(1)} %add.79), channel_id=1, source_target_pairs={{0,64},{8,72},{16,80},{24,88},{32,96},{40,104},{48,112},{56,120},{... | collective-permute-start | bytes 786440 | tf_op jit(solution)/shard_map/ppermute | solution.py:10
  135.9 30.0 %collective-permute-start.7 = (f32[256,256]{0,1:T(8,128)S(1)}, f32[256,256]{0,1:T(8,128)S(1)}, u32[]{:S(2)}, u32[]{:S(2)}) collective-permute-start(f32[256,256]{0,1:T(8,128)S(1)} %add.80), channel_id=1, source_target_pairs={{0,128},{8,136},{16,144},{24,152},{32,160},{40,168},{48,176},{56,1... | collective-permute-start | bytes 786440 | tf_op jit(solution)/shard_map/ppermute | solution.py:10
  166.0 9.2 %collective-permute-start.8 = (f32[256,256]{0,1:T(8,128)S(1)}, f32[256,256]{0,1:T(8,128)S(1)}, u32[]{:S(2)}, u32[]{:S(2)}) collective-permute-start(f32[256,256]{0,1:T(8,128)S(1)} %add.81), channel_id=1, source_target_pairs={{0,256},{8,264},{16,272},{24,280},{32,288},{40,296},{48,304},{56,3... | collective-permute-start | bytes 786440 | tf_op jit(solution)/shard_map/ppermute | solution.py:10
  175.3 469.7 %collective-permute-start.9 = (f32[256,256]{0,1:T(8,128)S(1)}, f32[256,256]{0,1:T(8,128)S(1)}, u32[]{:S(2)}, u32[]{:S(2)}) collective-permute-start(f32[256,256]{0,1:T(8,128)S(1)} %add.82), channel_id=1, source_target_pairs={{0,512},{8,520},{16,528},{24,536},{32,544},{40,552},{48,560},{56,5... | collective-permute-start | bytes 786440 | tf_op jit(solution)/shard_map/ppermute | solution.py:10
Sparse Core Ops, SparseCore 0:
  172.0 471.3 all-reduce.2
where the time goes:
time: 720 us; the launch traced here: 718 us
  waiting for transfers between devices  547 us (76%)
  starting transfers between devices  72.2 us (10%)
  other arithmetic  55 us (8%)
  matrix products  19.2 us (3%)
  between operations  16.3 us (2%)
  local copies, waits for them, and re-layouts  8.87 us (1%)
    psum x1, waiting for transfers between devices, spread(): return lax.psum(jnp.where(mine, array, jnp.zeros_like(array)), axis)  463 us
    ppermute x10, waiting for transfers between devices, partner(): lax.ppermute(array, axis, [(i, i ^ 1 << distance) for i in range(lax.axis...  83.4 us
    ppermute x10, starting transfers between devices, partner(): lax.ppermute(array, axis, [(i, i ^ 1 << distance) for i in range(lax.axis...  72.1 us
    another operation x6, other arithmetic, per_device(): lower = jnp.linalg.cholesky(gram)  34 us
    another operation x3, other arithmetic, per_device(): solved = jax.scipy.linalg.solve_triangular(lower, features.T, lower=True)  19.7 us
  transfers between devices with their start and end apart: 11, of which 10 were waited for; matrix products, arithmetic and copies ran while one was open for 0% of the time, Pallas kernels for 0%

commit v1 on v0

v1 whole, which is shorter than its diff:
```python
import functools
import math

import jax
import jax.numpy as jnp
import numpy as np
from jax import lax
from jax.experimental import pallas as pl
from jax.experimental.pallas import tpu as pltpu
from jax.sharding import PartitionSpec as P

MESH = pl.DeviceIdType.MESH
HIGHEST = lax.Precision.HIGHEST
LANES = 128
BLOCK = 16
TILE_ROWS = 256

TWO_PI_HI = float(np.float32(round(2 * math.pi * 2**15) / 2**15))
TWO_PI_LO = float(np.float32(2 * math.pi - TWO_PI_HI))


def half_sine_coefs():
    top = (math.pi * 1.001) ** 2
    nodes = top * (0.5 + 0.5 * np.cos((np.arange(64) + 0.5) * math.pi / 64))
    roots = np.sqrt(nodes)
    values = math.sqrt(2.0) * np.sin(roots / 2) / roots
    fit = np.polynomial.chebyshev.Chebyshev.fit(nodes, values, 5, domain=[0, top])
    power = fit.convert(kind=np.polynomial.Polynomial)
    return [float(c) for c in power.coef]


COEFS = half_sine_coefs()


def cosine(x):
    turns = jnp.round(x * (1.0 / (2 * math.pi)))
    r = (x - turns * TWO_PI_HI) - turns * TWO_PI_LO
    t = r * r
    poly = jnp.full_like(t, COEFS[-1])
    for c in COEFS[-2::-1]:
        poly = poly * t + c
    s = r * poly
    return 1.0 - s * s


def local_gram(x_ref, freqs_ref, phases_ref, weight_ref, stored_ref, root_ref, feat, me, rows_all):
    rows, feats = feat.shape
    total = None
    mine = jnp.where(root_ref[0] == me, 1.0, 0.0).astype(jnp.float32)
    run = stored_ref[0] * mine
    total = lax.dot_general(run, run, (((0,), (0,)), ((), ())), precision=HIGHEST, preferred_element_type=jnp.float32)
    acc = None
    step = 256
    for at in range(0, rows, step):
        proj = lax.dot_general(
            x_ref[:, at : at + step], freqs_ref[...], (((0,), (0,)), ((), ())),
            precision=HIGHEST, preferred_element_type=jnp.float32,
        ) + phases_ref[...]
        scales = []
        for sub in range(step // LANES):
            row = jnp.sqrt(weight_ref[pl.ds(at // LANES + sub, 1), :])
            scales.append(jnp.broadcast_to(row, (LANES, LANES)).T)
        scale = jnp.concatenate(scales, axis=0)
        scale = jnp.concatenate([scale] * (feats // LANES), axis=1)
        block = cosine(proj) * scale
        feat[at : at + step, :] = block
        part = lax.dot_general(block, block, (((0,), (0,)), ((), ())), precision=HIGHEST, preferred_element_type=jnp.float32)
        acc = part if acc is None else acc + part
    return total + acc * (1.0 / rows_all)


def reduce_kernel(sizes, rows_all, x_ref, freqs_ref, phases_ref, weight_ref, stored_ref, root_ref,
                  gram_ref, feat_out, feat, mine, theirs, half, parts, zparts, back, last,
                  feat_sem, core_send, core_recv, rs_send, rs_recv, z_send, z_recv, ag_send, ag_recv, end_send, end_recv):
    nx, nz, ny = sizes
    grp, leaf = lax.axis_index("grp"), lax.axis_index("leaf")
    core, z, x = lax.rem(grp, 2), lax.rem(grp // 2, nz), grp // (2 * nz)

    def at(x_, z_, core_, y_):
        return ((x_ * nz + z_) * 2 + core_, y_)

    other = at(x, z, 1 - core, leaf)
    plane = []
    for dx in range(nx):
        for dy in range(ny):
            if dx or dy:
                plane.append((min(dx, nx - dx) + min(dy, ny - dy), dx, dy))
    plane.sort(key=lambda t: -t[0])
    plane = [(lax.rem(x + dx, nx), lax.rem(leaf + dy, ny)) for _, dx, dy in plane]
    line = sorted(range(1, nz), key=lambda d: -min(d, nz - d))
    line = [lax.rem(z + dz, nz) for dz in line]

    barrier = pltpu.get_barrier_semaphore()
    pl.semaphore_signal(barrier, inc=1, device_id=other, device_id_type=MESH)
    for px, py in plane:
        pl.semaphore_signal(barrier, inc=1, device_id=at(px, z, core, py), device_id_type=MESH)
    for pz in line:
        pl.semaphore_signal(barrier, inc=1, device_id=at(x, pz, core, leaf), device_id_type=MESH)

    me = grp * ny + leaf
    gram = local_gram(x_ref, freqs_ref, phases_ref, weight_ref, stored_ref, root_ref, feat, me, rows_all)
    feat_copy = pltpu.make_async_copy(feat, feat_out, feat_sem)
    feat_copy.start()
    feats = gram.shape[0]
    chunks = feats // 8
    for side in range(2):
        mine[side] = gram[:, side * LANES : (side + 1) * LANES].reshape(chunks, 8, LANES)

    pl.semaphore_wait(barrier, 1 + len(plane) + len(line))

    swap = pltpu.make_async_remote_copy(mine.at[1 - core], theirs, core_send, core_recv, device_id=other, device_id_type=MESH)
    swap.start()
    swap.wait_recv()
    half[...] = mine[core] + theirs[...]

    spot = x * ny + leaf
    copies = []
    for n, (px, py) in enumerate(plane):
        there = px * ny + py
        copies.append(pltpu.make_async_remote_copy(
            half.at[there], parts.at[n], rs_send.at[n], rs_recv.at[n],
            device_id=at(px, z, core, py), device_id_type=MESH))
    for c in copies:
        c.start()
    total = half[spot]
    for n in reversed(range(len(copies))):
        copies[n].wait_recv()
        total = total + parts[n]

    zparts[z] = total
    lines = []
    for n, pz in enumerate(line):
        lines.append(pltpu.make_async_remote_copy(
            zparts.at[z], zparts.at[z], z_send.at[n], z_recv.at[n],
            device_id=at(x, pz, core, leaf), device_id_type=MESH))
    for c in lines:
        c.start()
    for c in lines:
        c.wait_recv()
    total = zparts[0]
    for k in range(1, nz):
        total = total + zparts[k]

    back[spot] = total
    spread = []
    for n, (px, py) in enumerate(plane):
        spread.append(pltpu.make_async_remote_copy(
            back.at[spot], back.at[spot], ag_send.at[n], ag_recv.at[n],
            device_id=at(px, z, core, py), device_id_type=MESH))
    for c in spread:
        c.start()
    for c in spread:
        c.wait_recv()

    end = pltpu.make_async_remote_copy(back, last, end_send, end_recv, device_id=other, device_id_type=MESH)
    end.start()
    for c in [swap] + copies + lines + spread:
        c.wait_send()
    own = back[...].reshape(feats, LANES)
    end.wait_recv()
    got = last[...].reshape(feats, LANES)
    first = core == 0
    gram_ref[:, :LANES] = jnp.where(first, own, got)
    gram_ref[:, LANES:] = jnp.where(first, got, own)
    end.wait_send()
    feat_copy.wait()


def eliminate(a, factor_ref, inverse, block):
    n = a.shape[0]
    groups = block // 8
    sub8 = lax.broadcasted_iota(jnp.int32, (8, LANES), 0)
    rows_of = lax.broadcasted_iota(jnp.int32, (block, n), 0)
    cols_of = lax.broadcasted_iota(jnp.int32, (block, n), 1)
    ntile = n // LANES
    for r0 in range(0, n, block):
        panel = a[r0 : r0 + block, :]
        col = []
        for j in range(block):
            wide = jnp.broadcast_to(panel[:, r0 + j : r0 + j + 1], (block, LANES))
            col.append([wide[8 * g : 8 * g + 8] for g in range(groups)])
        base = (r0 // LANES) * LANES
        lane0 = r0 - base
        eye = (cols_of[:, :LANES] == rows_of[:, :LANES] + lane0).astype(jnp.float32)
        row = [[panel[8 * g : 8 * g + 8, LANES * t : LANES * t + LANES] for g in range(groups)] for t in range(ntile)]
        row.append([eye[8 * g : 8 * g + 8] for g in range(groups)])
        pivots = [None] * groups
        for k in range(block):
            gk, sk = divmod(k, 8)
            pivot = jnp.broadcast_to(col[k][gk][sk : sk + 1], (8, LANES))
            pivots[gk] = pivot if sk == 0 else jnp.where(sub8 >= sk, pivot, pivots[gk])
            if k == block - 1:
                break
            inv = 1.0 / pivot
            mult = {}
            for g in range(gk, groups):
                if g == gk and sk == 7:
                    continue
                m = col[k][g] * inv
                if g == gk:
                    m = jnp.where(sub8 > sk, m, 0.0)
                mult[g] = m
            for j in range(k + 1, block):
                lead = jnp.broadcast_to(col[j][gk][sk : sk + 1], (8, LANES))
                for g, m in mult.items():
                    col[j][g] = col[j][g] - m * lead
            for part in row:
                lead = jnp.broadcast_to(part[gk][sk : sk + 1], (8, LANES))
                for g, m in mult.items():
                    part[g] = part[g] - m * lead
        scale = [lax.rsqrt(p) for p in pivots]
        scaled = [jnp.concatenate([part[g] * scale[g] for g in range(groups)], axis=0) for part in row]
        full = jnp.concatenate(scaled[:ntile], axis=1)
        unit = jnp.concatenate([scaled[ntile]] * ntile, axis=1)
        upper = jnp.where(cols_of >= rows_of + r0, full, 0.0)
        factor_ref[r0 : r0 + block, :] = upper
        lower = jnp.where(cols_of < r0, full, jnp.where(cols_of <= rows_of + r0, unit, 0.0))
        inverse[r0 : r0 + block, :] = lower
        r1 = r0 + block
        if r1 < n:
            both = jnp.where(cols_of >= r1, full, lower)
            left = upper.T[r1:, :]
            drop = lax.dot_general(left, both, (((1,), (0,)), ((), ())), precision=HIGHEST, preferred_element_type=jnp.float32)
            old = a[r1:, :]
            cols_rest = lax.broadcasted_iota(jnp.int32, (n - r1, n), 1)
            fresh = (cols_rest >= r0) & (cols_rest < r1)
            a[r1:, :] = jnp.where(fresh, 0.0, old) - drop


def basis_kernel(gram_ref, feat_in, factor_ref, basis_out, a, inverse, feat, out, in_sem, out_sem):
    load = pltpu.make_async_copy(feat_in, feat, in_sem)
    load.start()
    a[...] = gram_ref[...]
    eliminate(a, factor_ref, inverse, BLOCK)
    right = inverse[...].T
    load.wait()
    rows = feat.shape[0]
    copies = []
    for n, at in enumerate(range(0, rows, TILE_ROWS)):
        tile = pl.ds(at, TILE_ROWS)
        out[tile, :] = jnp.dot(feat[tile, :], right, precision=HIGHEST, preferred_element_type=jnp.float32)
        c = pltpu.make_async_copy(out.at[tile, :], basis_out.at[tile, :], out_sem.at[n])
        c.start()
        copies.append(c)
    for c in copies:
        c.wait()


VMEM = functools.partial(pl.BlockSpec, memory_space=pltpu.VMEM)
ANY = functools.partial(pl.BlockSpec, memory_space=pl.ANY)


def run_basis(gram, features):
    rows, feats = features.shape
    f32 = jnp.float32
    return pl.pallas_call(
        basis_kernel,
        out_shape=(jax.ShapeDtypeStruct((feats, feats), f32), jax.ShapeDtypeStruct((rows, feats), f32)),
        in_specs=[VMEM(), ANY()],
        out_specs=(VMEM(), ANY()),
        scratch_shapes=[
            pltpu.VMEM((feats, feats), f32),
            pltpu.VMEM((feats, feats), f32),
            pltpu.VMEM((rows, feats), f32),
            pltpu.VMEM((rows, feats), f32),
            pltpu.SemaphoreType.DMA,
            pltpu.SemaphoreType.DMA((rows // TILE_ROWS,)),
        ],
        compiler_params=pltpu.CompilerParams(vmem_limit_bytes=32 * 2**20),
        name="basis",
    )(gram, features)


def per_device(sizes, rows_all, inputs, freqs, phases, sample_weight, stored, root):
    rows, feats = inputs.shape[0], freqs.shape[1]
    nx, nz, ny = sizes
    f32 = jnp.float32
    nplane, nline = nx * ny - 1, nz - 1
    chunks = feats // 8
    dma = pltpu.SemaphoreType.DMA
    gram, features = pl.pallas_call(
        functools.partial(reduce_kernel, sizes, rows_all),
        out_shape=(jax.ShapeDtypeStruct((feats, feats), f32), jax.ShapeDtypeStruct((rows, feats), f32)),
        in_specs=[VMEM()] * 5 + [pl.BlockSpec(memory_space=pltpu.SMEM)],
        out_specs=(VMEM(), ANY()),
        scratch_shapes=[
            pltpu.VMEM((rows, feats), f32),
            pltpu.VMEM((2, chunks, 8, LANES), f32),
            pltpu.VMEM((chunks, 8, LANES), f32),
            pltpu.VMEM((chunks, 8, LANES), f32),
            pltpu.VMEM((nplane, 8, LANES), f32),
            pltpu.VMEM((nz, 8, LANES), f32),
            pltpu.VMEM((chunks, 8, LANES), f32),
            pltpu.VMEM((chunks, 8, LANES), f32),
            dma, dma, dma,
            dma((nplane,)), dma((nplane,)),
            dma((nline,)), dma((nline,)),
            dma((nplane,)), dma((nplane,)),
            dma, dma,
        ],
        compiler_params=pltpu.CompilerParams(collective_id=0, has_side_effects=True, vmem_limit_bytes=32 * 2**20),
        name="reduce",
    )(inputs.T, freqs, phases[None, :], sample_weight.reshape(rows // LANES, LANES), stored, root)
    return run_basis(gram, features)


def solution(mesh):
    groups, leaves = mesh.shape["grp"], mesh.shape["leaf"]
    nx = 256 // 8 // leaves
    sizes = (nx, groups // 2 // nx, leaves)
    return jax.shard_map(
        lambda inputs, *rest: per_device(sizes, inputs.shape[0] * groups * leaves, inputs, *rest),
        mesh=mesh,
        in_specs=(
            P(("grp", "leaf"), None),
            P(),
            P(),
            P(("grp", "leaf")),
            P(("grp", "leaf"), None, None),
            P(),
        ),
        out_specs=(P(), P(("grp", "leaf"), None)),
        check_vma=False,
    )
```

time: 720 us -> 68.5 us (0.10)
  waiting for transfers between devices: 547 us -> 0 us
  starting transfers between devices: 72.2 us -> 0 us
  Pallas kernels: 0 us -> 62.5 us
  other arithmetic: 55 us -> 0 us
  matrix products: 19.2 us -> 0 us
  between operations: 16.3 us -> 0.81 us
    psum x1 -> x0, waiting for transfers between devices: 463 us -> none  [spread(): return lax.psum(jnp.where(mine, array, jnp.zeros_like(array)), axis)]
    ppermute x10 -> x0, waiting for transfers between devices: 83.4 us -> none  [partner(): lax.ppermute(array, axis, [(i, i ^ 1 << distance) for i in range(lax.axis...]
    ppermute x10 -> x0, starting transfers between devices: 72.1 us -> none  [partner(): lax.ppermute(array, axis, [(i, i ^ 1 << distance) for i in range(lax.axis...]
    pallas_call x0 -> x2, Pallas kernels: none -> 62.5 us  [the longest x1 48.7 us: per_device(): pl.pallas_call(functools.partial(reduce_kernel, sizes, rows_all), out_sha...]
    another operation x9 -> x0, other arithmetic: 53.7 us -> none  [the longest x6 34 us: per_device(): lower = jnp.linalg.cholesky(gram)]
    dot_general x3 -> x0, matrix products: 14.8 us -> none  [the longest x1 9.54 us: per_device(): jnp.dot(inputs, freqs, precision=lax.Precision.HIGHEST) + phases[None, :]]
  transfers between devices with their start and end apart: 11 -> 0, of which waited for: 10 -> 0; matrix products, arithmetic and copies ran while one was open for 0% -> 0% of each run, Pallas kernels for 0% -> 0%
where the time goes in v1:
time: 68.5 us; the launch traced here: 68.2 us
  Pallas kernels  62.5 us (91%)
  local copies, waits for them, and re-layouts  4.88 us (7%)
  between operations  0.81 us (1%)
    pallas_call x1, Pallas kernels, per_device(): pl.pallas_call(functools.partial(reduce_kernel, sizes, rows_all), out_sha...  48.7 us
    pallas_call x1, Pallas kernels, run_basis(): pl.pallas_call(basis_kernel, out_shape=(jax.ShapeDtypeStruct((feats, feat...  13.8 us
    unnamed x12, local copies, waits for them, and re-layouts  4.88 us

profile of v1, /device:TPU:1, one launch (start us, length us, event | category | flops | bytes accessed | tf_op | source)
XLA Modules:
  0.0 68.2 jit_solution(12224406957316836342)
XLA Ops:
  0.6 0.0 copy-start
  0.6 1.0 %copy-done = f32[2048,64]{0,1:T(8,128)S(1)} copy-done((f32[2048,64]{0,1:T(8,128)S(1)}, f32[2048,64]{0,1:T(8,128)}, u32[]{:S(2)}) %copy-start) | copy-done | bytes 524312
  1.7 0.0 copy-start.1
  1.7 0.9 %copy-done.1 = f32[1,256,256]{2,1,0:T(8,128)S(1)} copy-done((f32[1,256,256]{2,1,0:T(8,128)S(1)}, f32[1,256,256]{2,1,0:T(8,128)}, u32[]{:S(2)}) %copy-start.1) | copy-done | bytes 262168
  2.6 0.0 copy-start.2
  2.6 0.8 %copy-done.2 = f32[64,256]{1,0:T(8,128)S(1)} copy-done((f32[64,256]{1,0:T(8,128)S(1)}, f32[64,256]{1,0:T(8,128)}, u32[]{:S(2)}) %copy-start.2) | copy-done | bytes 65560
  3.5 0.0 copy-start.3
  3.5 0.7 %copy-done.3 = f32[2048]{0:T(1024)S(1)} copy-done((f32[2048]{0:T(1024)S(1)}, f32[2048]{0:T(1024)}, u32[]{:S(2)}) %copy-start.3) | copy-done | bytes 8216
  4.2 0.0 copy-start.4
  4.2 0.7 %copy-done.4 = s32[1024]{0:T(1024)S(1)} copy-done((s32[1024]{0:T(1024)S(1)}, s32[1024]{0:T(1024)}, u32[]{:S(2)}) %copy-start.4) | copy-done | bytes 4120
  4.8 0.0 copy-start.5
  4.9 0.7 copy-done.5
  5.5 48.7 %reduce.1 = (f32[256,256]{1,0:T(8,128)S(1)}, f32[2048,256]{1,0:T(8,128)S(1)}) custom-call(f32[64,2048]{1,0:T(8,128)S(1)} %bitcast.3, f32[64,256]{1,0:T(8,128)S(1)} %copy-done.2, f32[1,256]{1,0:T(1,128)S(1)} %bitcast.5, f32[16,128]{1,0:T(8,128)S(1)} %bitcast.4, f32[1,256,256]{2,1,0:T(8,128)S(1)} %copy-done.1, s32[1024]{0:T(1024)S(1)} %copy-done.4), custom_call_target="tpu_custom_call" | custom-call | tf_op jit(solution)/shard_map/reduce/pallas_call | solution.py:281
  54.2 13.8 %basis.1 = (f32[256,256]{1,0:T(8,128)}, f32[2048,256]{1,0:T(8,128)}) custom-call(f32[256,256]{1,0:T(8,128)S(1)} %get-tuple-element.4.gram_ref, f32[2048,256]{1,0:T(8,128)S(1)} %get-tuple-element.5.feat_in), custom_call_target="tpu_custom_call" | custom-call | tf_op jit(solution)/shard_map/basis/pallas_call | solution.py:256
Async XLA Ops:
  0.6 1.0 %copy-start = (f32[2048,64]{0,1:T(8,128)S(1)}, f32[2048,64]{0,1:T(8,128)}, u32[]{:S(2)}) copy-start(f32[2048,64]{0,1:T(8,128)} %param.6) | copy-start | bytes 1572868
  1.7 0.9 %copy-start.1 = (f32[1,256,256]{2,1,0:T(8,128)S(1)}, f32[1,256,256]{2,1,0:T(8,128)}, u32[]{:S(2)}) copy-start(f32[1,256,256]{2,1,0:T(8,128)} %stored_ref.1) | copy-start | bytes 786436
  2.6 0.8 %copy-start.2 = (f32[64,256]{1,0:T(8,128)S(1)}, f32[64,256]{1,0:T(8,128)}, u32[]{:S(2)}) copy-start(f32[64,256]{1,0:T(8,128)} %freqs_ref.1) | copy-start | bytes 196612
  3.5 0.7 %copy-start.3 = (f32[2048]{0:T(1024)S(1)}, f32[2048]{0:T(1024)}, u32[]{:S(2)}) copy-start(f32[2048]{0:T(1024)} %param.9) | copy-start | bytes 24580
  4.2 0.7 %copy-start.4 = (s32[1024]{0:T(1024)S(1)}, s32[1024]{0:T(1024)}, u32[]{:S(2)}) copy-start(s32[1024]{0:T(1024)} %root_ref.1) | copy-start | bytes 12292
  4.8 0.7 copy-start.5

commit v2 on v1

--- a/solution.py
+++ b/solution.py
@@ -14,6 +14,7 @@
 LANES = 128
 BLOCK = 16
 TILE_ROWS = 256
+STEP_ROWS = 512
 
 TWO_PI_HI = float(np.float32(round(2 * math.pi * 2**15) / 2**15))
 TWO_PI_LO = float(np.float32(2 * math.pi - TWO_PI_HI))
@@ -43,35 +44,50 @@
     return 1.0 - s * s
 
 
+def pieces(x):
+    high = x.astype(jnp.bfloat16)
+    rest = x - high.astype(jnp.float32)
+    middle = rest.astype(jnp.bfloat16)
+    return high, middle, (rest - middle.astype(jnp.float32)).astype(jnp.bfloat16)
+
+
 def local_gram(x_ref, freqs_ref, phases_ref, weight_ref, stored_ref, root_ref, feat, me, rows_all):
     rows, feats = feat.shape
-    total = None
-    mine = jnp.where(root_ref[0] == me, 1.0, 0.0).astype(jnp.float32)
-    run = stored_ref[0] * mine
-    total = lax.dot_general(run, run, (((0,), (0,)), ((), ())), precision=HIGHEST, preferred_element_type=jnp.float32)
+    down = (((0,), (0,)), ((), ()))
+    high, middle, low = pieces(freqs_ref[...])
+    freqs = jnp.concatenate([high, middle, high, middle, low, high], axis=0)
     acc = None
-    step = 256
-    for at in range(0, rows, step):
-        proj = lax.dot_general(
-            x_ref[:, at : at + step], freqs_ref[...], (((0,), (0,)), ((), ())),
-            precision=HIGHEST, preferred_element_type=jnp.float32,
-        ) + phases_ref[...]
+    for at in range(0, rows, STEP_ROWS):
+        high, middle, low = pieces(x_ref[:, at : at + STEP_ROWS])
+        x = jnp.concatenate([high, high, middle, middle, high, low], axis=0)
+        proj = lax.dot_general(x, freqs, down, preferred_element_type=jnp.float32) + phases_ref[...]
         scales = []
-        for sub in range(step // LANES):
+        for sub in range(STEP_ROWS // LANES):
             row = jnp.sqrt(weight_ref[pl.ds(at // LANES + sub, 1), :])
             scales.append(jnp.broadcast_to(row, (LANES, LANES)).T)
         scale = jnp.concatenate(scales, axis=0)
         scale = jnp.concatenate([scale] * (feats // LANES), axis=1)
         block = cosine(proj) * scale
-        feat[at : at + step, :] = block
-        part = lax.dot_general(block, block, (((0,), (0,)), ((), ())), precision=HIGHEST, preferred_element_type=jnp.float32)
+        feat[at : at + STEP_ROWS, :] = block
+        part = lax.dot_general(block, block, down, precision=HIGHEST, preferred_element_type=jnp.float32)
         acc = part if acc is None else acc + part
-    return total + acc * (1.0 / rows_all)
-
-
-def reduce_kernel(sizes, rows_all, x_ref, freqs_ref, phases_ref, weight_ref, stored_ref, root_ref,
-                  gram_ref, feat_out, feat, mine, theirs, half, parts, zparts, back, last,
-                  feat_sem, core_send, core_recv, rs_send, rs_recv, z_send, z_recv, ag_send, ag_recv, end_send, end_recv):
+    run = stored_ref[0] * jnp.where(root_ref[0] == me, 1.0, 0.0).astype(jnp.float32)
+    running = lax.dot_general(run, run, down, precision=HIGHEST, preferred_element_type=jnp.float32)
+    return running + acc * (1.0 / rows_all)
+
+
+def reduce_kernel(sizes, rows_all, *refs):
+    sources, refs = refs[:6], refs[6:]
+    loaded, load_sem, refs = refs[2:8], refs[8], refs[:2] + refs[9:]
+    loads = [pltpu.make_async_copy(s, d, load_sem.at[n]) for n, (s, d) in enumerate(zip(sources, loaded))]
+    for c in loads:
+        c.start()
+    reduce_loaded(sizes, rows_all, loads, *loaded, *refs)
+
+
+def reduce_loaded(sizes, rows_all, loads, x_ref, freqs_ref, phases_ref, weight_ref, stored_ref, root_ref,
+                  gram_out, feat_out, feat, mine, theirs, half, parts, zparts, back,
+                  feat_sem, core_send, core_recv, rs_send, rs_recv, z_send, z_recv, ag_send, ag_recv, end_send, end_recv, keep_sem):
     nx, nz, ny = sizes
     grp, leaf = lax.axis_index("grp"), lax.axis_index("leaf")
     core, z, x = lax.rem(grp, 2), lax.rem(grp // 2, nz), grp // (2 * nz)
@@ -98,6 +114,8 @@
         pl.semaphore_signal(barrier, inc=1, device_id=at(x, pz, core, leaf), device_id_type=MESH)
 
     me = grp * ny + leaf
+    for c in loads:
+        c.wait()
     gram = local_gram(x_ref, freqs_ref, phases_ref, weight_ref, stored_ref, root_ref, feat, me, rows_all)
     feat_copy = pltpu.make_async_copy(feat, feat_out, feat_sem)
     feat_copy.start()
@@ -152,45 +170,61 @@
     for c in spread:
         c.wait_recv()
 
-    end = pltpu.make_async_remote_copy(back, last, end_send, end_recv, device_id=other, device_id_type=MESH)
+    end = pltpu.make_async_remote_copy(back, gram_out.at[core], end_send, end_recv, device_id=other, device_id_type=MESH)
     end.start()
+    keep = pltpu.make_async_copy(back, gram_out.at[core], keep_sem)
+    keep.start()
     for c in [swap] + copies + lines + spread:
         c.wait_send()
-    own = back[...].reshape(feats, LANES)
-    end.wait_recv()
-    got = last[...].reshape(feats, LANES)
-    first = core == 0
-    gram_ref[:, :LANES] = jnp.where(first, own, got)
-    gram_ref[:, LANES:] = jnp.where(first, got, own)
-    end.wait_send()
     feat_copy.wait()
-
-
-def eliminate(a, factor_ref, inverse, block):
+    keep.wait()
+    end.wait()
+
+
+def columns(values, first, block):
+    out = []
+    for j in range(block):
+        wide = jnp.broadcast_to(values[:, first + j : first + j + 1], (block, LANES))
+        out.append([wide[8 * g : 8 * g + 8] for g in range(block // 8)])
+    return out
+
+
+def eliminate(a, factor, inverse, block):
     n = a.shape[0]
     groups = block // 8
+    ntile = n // LANES
     sub8 = lax.broadcasted_iota(jnp.int32, (8, LANES), 0)
     rows_of = lax.broadcasted_iota(jnp.int32, (block, n), 0)
     cols_of = lax.broadcasted_iota(jnp.int32, (block, n), 1)
-    ntile = n // LANES
+
+    def spread(part, g, s):
+        return jnp.broadcast_to(part[g][s : s + 1], (8, LANES))
+
+    def split(values):
+        return [[values[8 * g : 8 * g + 8, LANES * t : LANES * t + LANES] for g in range(groups)] for t in range(values.shape[1] // LANES)]
+
+    def within(cols, lo):
+        return (cols >= lo) & (cols < lo + block)
+
+    panel = a[0:block, :]
+    drop = None
     for r0 in range(0, n, block):
-        panel = a[r0 : r0 + block, :]
-        col = []
-        for j in range(block):
-            wide = jnp.broadcast_to(panel[:, r0 + j : r0 + j + 1], (block, LANES))
-            col.append([wide[8 * g : 8 * g + 8] for g in range(groups)])
-        base = (r0 // LANES) * LANES
-        lane0 = r0 - base
+        r1, r2 = r0 + block, r0 + 2 * block
+        ahead = r1 < n
+        col = columns(panel, r0, block)
+        if ahead:
+            base = (r1 // LANES) * LANES
+            turned = panel[:, base : base + LANES].T[r1 - base : r2 - base, :]
+            below = columns(turned, 0, block)
+        lane0 = r0 % LANES
         eye = (cols_of[:, :LANES] == rows_of[:, :LANES] + lane0).astype(jnp.float32)
-        row = [[panel[8 * g : 8 * g + 8, LANES * t : LANES * t + LANES] for g in range(groups)] for t in range(ntile)]
-        row.append([eye[8 * g : 8 * g + 8] for g in range(groups)])
+        row = split(panel) + split(eye)
+        gone = [[None] * groups for _ in row]
         pivots = [None] * groups
         for k in range(block):
             gk, sk = divmod(k, 8)
-            pivot = jnp.broadcast_to(col[k][gk][sk : sk + 1], (8, LANES))
+            pivot = spread(col[k], gk, sk)
             pivots[gk] = pivot if sk == 0 else jnp.where(sub8 >= sk, pivot, pivots[gk])
-            if k == block - 1:
-                break
             inv = 1.0 / pivot
             mult = {}
             for g in range(gk, groups):
@@ -200,42 +234,57 @@
                 if g == gk:
                     m = jnp.where(sub8 > sk, m, 0.0)
                 mult[g] = m
+            under = [below[k][g] * inv for g in range(groups)] if ahead else []
             for j in range(k + 1, block):
-                lead = jnp.broadcast_to(col[j][gk][sk : sk + 1], (8, LANES))
+                lead = spread(col[j], gk, sk)
                 for g, m in mult.items():
                     col[j][g] = col[j][g] - m * lead
-            for part in row:
-                lead = jnp.broadcast_to(part[gk][sk : sk + 1], (8, LANES))
+                for g, m in enumerate(under):
+                    below[j][g] = below[j][g] - m * lead
+            for part, taken in zip(row, gone):
+                lead = spread(part, gk, sk)
                 for g, m in mult.items():
                     part[g] = part[g] - m * lead
+                for g, m in enumerate(under):
+                    taken[g] = m * lead if k == 0 else taken[g] + m * lead
         scale = [lax.rsqrt(p) for p in pivots]
         scaled = [jnp.concatenate([part[g] * scale[g] for g in range(groups)], axis=0) for part in row]
         full = jnp.concatenate(scaled[:ntile], axis=1)
         unit = jnp.concatenate([scaled[ntile]] * ntile, axis=1)
         upper = jnp.where(cols_of >= rows_of + r0, full, 0.0)
-        factor_ref[r0 : r0 + block, :] = upper
+        factor[r0:r1, :] = upper
         lower = jnp.where(cols_of < r0, full, jnp.where(cols_of <= rows_of + r0, unit, 0.0))
-        inverse[r0 : r0 + block, :] = lower
-        r1 = r0 + block
-        if r1 < n:
+        inverse[r0:r1, :] = lower
+        if drop is not None and ahead:
+            cols_rest = lax.broadcasted_iota(jnp.int32, (n - r1, n), 1)
+            a[r1:, :] = jnp.where(within(cols_rest, r0 - block), 0.0, a[r1:, :]) - drop
+        if r2 < n:
             both = jnp.where(cols_of >= r1, full, lower)
-            left = upper.T[r1:, :]
+            left = upper.T[r2:, :]
             drop = lax.dot_general(left, both, (((1,), (0,)), ((), ())), precision=HIGHEST, preferred_element_type=jnp.float32)
-            old = a[r1:, :]
-            cols_rest = lax.broadcasted_iota(jnp.int32, (n - r1, n), 1)
-            fresh = (cols_rest >= r0) & (cols_rest < r1)
-            a[r1:, :] = jnp.where(fresh, 0.0, old) - drop
-
-
-def basis_kernel(gram_ref, feat_in, factor_ref, basis_out, a, inverse, feat, out, in_sem, out_sem):
-    load = pltpu.make_async_copy(feat_in, feat, in_sem)
+        if ahead:
+            taken = [jnp.concatenate(part, axis=0) for part in gone]
+            rest = jnp.concatenate(taken[:ntile], axis=1)
+            own = jnp.concatenate([taken[ntile]] * ntile, axis=1)
+            here = within(cols_of, r0)
+            panel = jnp.where(here, 0.0, a[r1:r2, :]) - jnp.where(here, own, rest)
+
+
+def basis_kernel(gram_in, feat_in, factor_out, basis_out, gram, a, factor, inverse, feat, out, in_sem, factor_sem, out_sem):
+    first = pltpu.make_async_copy(gram_in, gram, in_sem.at[0])
+    first.start()
+    load = pltpu.make_async_copy(feat_in, feat, in_sem.at[1])
     load.start()
-    a[...] = gram_ref[...]
-    eliminate(a, factor_ref, inverse, BLOCK)
+    first.wait()
+    feats = a.shape[0]
+    for side in range(2):
+        a[:, side * LANES : (side + 1) * LANES] = gram[side].reshape(feats, LANES)
+    eliminate(a, factor, inverse, BLOCK)
+    copies = [pltpu.make_async_copy(factor, factor_out, factor_sem)]
+    copies[0].start()
     right = inverse[...].T
     load.wait()
     rows = feat.shape[0]
-    copies = []
     for n, at in enumerate(range(0, rows, TILE_ROWS)):
         tile = pl.ds(at, TILE_ROWS)
         out[tile, :] = jnp.dot(feat[tile, :], right, precision=HIGHEST, preferred_element_type=jnp.float32)
@@ -247,26 +296,28 @@
 
 
 VMEM = functools.partial(pl.BlockSpec, memory_space=pltpu.VMEM)
-ANY = functools.partial(pl.BlockSpec, memory_space=pl.ANY)
+HBM = functools.partial(pl.BlockSpec, memory_space=pltpu.HBM)
 
 
 def run_basis(gram, features):
     rows, feats = features.shape
     f32 = jnp.float32
+    square = pltpu.VMEM((feats, feats), f32)
     return pl.pallas_call(
         basis_kernel,
         out_shape=(jax.ShapeDtypeStruct((feats, feats), f32), jax.ShapeDtypeStruct((rows, feats), f32)),
-        in_specs=[VMEM(), ANY()],
-        out_specs=(VMEM(), ANY()),
+        in_specs=[HBM(), HBM()],
+        out_specs=(HBM(), HBM()),
         scratch_shapes=[
-            pltpu.VMEM((feats, feats), f32),
-            pltpu.VMEM((feats, feats), f32),
+            pltpu.VMEM(gram.shape, f32),
+            square, square, square,
             pltpu.VMEM((rows, feats), f32),
             pltpu.VMEM((rows, feats), f32),
+            pltpu.SemaphoreType.DMA((2,)),
             pltpu.SemaphoreType.DMA,
             pltpu.SemaphoreType.DMA((rows // TILE_ROWS,)),
         ],
-        compiler_params=pltpu.CompilerParams(vmem_limit_bytes=32 * 2**20),
+        compiler_params=pltpu.CompilerParams(vmem_limit_bytes=60 * 2**20),
         name="basis",
     )(gram, features)
 
@@ -280,10 +331,17 @@
     dma = pltpu.SemaphoreType.DMA
     gram, features = pl.pallas_call(
         functools.partial(reduce_kernel, sizes, rows_all),
-        out_shape=(jax.ShapeDtypeStruct((feats, feats), f32), jax.ShapeDtypeStruct((rows, feats), f32)),
-        in_specs=[VMEM()] * 5 + [pl.BlockSpec(memory_space=pltpu.SMEM)],
-        out_specs=(VMEM(), ANY()),
+        out_shape=(jax.ShapeDtypeStruct((2, chunks, 8, LANES), f32), jax.ShapeDtypeStruct((rows, feats), f32)),
+        in_specs=[HBM()] * 6,
+        out_specs=(HBM(), HBM()),
         scratch_shapes=[
+            pltpu.VMEM((inputs.shape[1], rows), f32),
+            pltpu.VMEM(freqs.shape, f32),
+            pltpu.VMEM((1, feats), f32),
+            pltpu.VMEM((rows // LANES, LANES), f32),
+            pltpu.VMEM(stored.shape, f32),
+            pltpu.SMEM(root.shape, jnp.int32),
+            dma((6,)),
             pltpu.VMEM((rows, feats), f32),
             pltpu.VMEM((2, chunks, 8, LANES), f32),
             pltpu.VMEM((chunks, 8, LANES), f32),
@@ -291,14 +349,13 @@
             pltpu.VMEM((nplane, 8, LANES), f32),
             pltpu.VMEM((nz, 8, LANES), f32),
             pltpu.VMEM((chunks, 8, LANES), f32),
-            pltpu.VMEM((chunks, 8, LANES), f32),
             dma, dma, dma,
             dma((nplane,)), dma((nplane,)),
             dma((nline,)), dma((nline,)),
             dma((nplane,)), dma((nplane,)),
-            dma, dma,
+            dma, dma, dma,
         ],
-        compiler_params=pltpu.CompilerParams(collective_id=0, has_side_effects=True, vmem_limit_bytes=32 * 2**20),
+        compiler_params=pltpu.CompilerParams(collective_id=0, has_side_effects=True, vmem_limit_bytes=60 * 2**20),
         name="reduce",
     )(inputs.T, freqs, phases[None, :], sample_weight.reshape(rows // LANES, LANES), stored, root)
     return run_basis(gram, features)

time: 68.5 us -> 60.3 us (0.88)
  local copies, waits for them, and re-layouts: 4.88 us -> 0 us
  Pallas kernels: 62.5 us -> 59.5 us
    unnamed x12 -> x0, local copies, waits for them, and re-layouts: 4.88 us -> none
    pallas_call x1, Pallas kernels: 13.8 us -> 11.2 us  [run_basis(): pl.pallas_call(basis_kernel, out_shape=(jax.ShapeDtypeStruct((feats, feat...]
where the time goes in v2:
time: 60.3 us; the launch traced here: 60.1 us
  Pallas kernels  59.5 us (99%)
  between operations  0.64 us (1%)
    pallas_call x1, Pallas kernels, per_device(): pl.pallas_call(functools.partial(reduce_kernel, sizes, rows_all), out_sha...  48.3 us
    pallas_call x1, Pallas kernels, run_basis(): pl.pallas_call(basis_kernel, out_shape=(jax.ShapeDtypeStruct((feats, feat...  11.2 us

profile of v2, /device:TPU:1, one launch (start us, length us, event | category | flops | bytes accessed | tf_op | source)
XLA Modules:
  0.0 60.1 jit_solution(15008948452203681013)
XLA Ops:
  0.6 48.3 %reduce.1 = (f32[2,32,8,128]{3,2,1,0:T(8,128)}, f32[2048,256]{1,0:T(8,128)}) custom-call(f32[64,2048]{1,0:T(8,128)} %bitcast.3, f32[64,256]{1,0:T(8,128)} %refs_1_.1, f32[1,256]{1,0:T(1,128)} %bitcast.5, f32[16,128]{1,0:T(8,128)} %bitcast.4, f32[1,256,256]{2,1,0:T(8,128)} %refs_4_.1, s32[1024]{0:T(1024)} %refs_5_.1), custom_call_target="tpu_custom_call" | custom-call | tf_op jit(solution)/shard_map/reduce/pallas_call | solution.py:332
  49.0 11.2 %basis.1 = (f32[256,256]{1,0:T(8,128)}, f32[2048,256]{1,0:T(8,128)}) custom-call(f32[2,32,8,128]{3,2,1,0:T(8,128)} %get-tuple-element.4.gram_in, f32[2048,256]{1,0:T(8,128)} %get-tuple-element.5.feat_in), custom_call_target="tpu_custom_call" | custom-call | tf_op jit(solution)/shard_map/basis/pallas_call | solution.py:306

commit v3 on v2

--- a/solution.py
+++ b/solution.py
@@ -14,7 +14,8 @@
 LANES = 128
 BLOCK = 16
 TILE_ROWS = 256
-STEP_ROWS = 512
+STEP_ROWS = 1024
+CHUNK_ROWS = 5
 
 TWO_PI_HI = float(np.float32(round(2 * math.pi * 2**15) / 2**15))
 TWO_PI_LO = float(np.float32(2 * math.pi - TWO_PI_HI))
@@ -69,11 +70,44 @@
         scale = jnp.concatenate([scale] * (feats // LANES), axis=1)
         block = cosine(proj) * scale
         feat[at : at + STEP_ROWS, :] = block
-        part = lax.dot_general(block, block, down, precision=HIGHEST, preferred_element_type=jnp.float32)
-        acc = part if acc is None else acc + part
+        high, middle, low = pieces(block)
+        part = lax.dot_general(high, jnp.concatenate([high, middle, low], axis=1), down, preferred_element_type=jnp.float32)
+        cross = part[:, feats : 2 * feats] + part[:, 2 * feats :]
+        even = part[:, :feats] + lax.dot_general(middle, middle, down, preferred_element_type=jnp.float32)
+        acc = (even, cross) if acc is None else (acc[0] + even, acc[1] + cross)
     run = stored_ref[0] * jnp.where(root_ref[0] == me, 1.0, 0.0).astype(jnp.float32)
     running = lax.dot_general(run, run, down, precision=HIGHEST, preferred_element_type=jnp.float32)
-    return running + acc * (1.0 / rows_all)
+    return running + (acc[0] + (acc[1] + acc[1].T)) * (1.0 / rows_all)
+
+
+def triangles():
+    row = lax.broadcasted_iota(jnp.int32, (LANES, LANES), 0)
+    col = lax.broadcasted_iota(jnp.int32, (LANES, LANES), 1)
+    return row, col
+
+
+def pack(gram, mine):
+    row, col = triangles()
+    last = gram[LANES:, LANES:]
+    squares = [jnp.where(row <= col, gram[:LANES, :LANES], last), gram[:LANES, LANES:]]
+    diagonal = jnp.sum(jnp.where(row == col, last, 0.0), axis=0, keepdims=True)
+    for side, square in enumerate(squares):
+        for n in range(LANES // 4):
+            mine[side, n, 0:4, :] = square[4 * n : 4 * n + 4]
+            if side or n:
+                mine[side, n, 4:5, :] = jnp.zeros((1, LANES), jnp.float32)
+    mine[0, 0, 4:5, :] = diagonal
+
+
+def unpack(chunks, a):
+    row, col = triangles()
+    squares = [jnp.concatenate([chunks[side, n, 0:4, :] for n in range(LANES // 4)], axis=0) for side in range(2)]
+    mixed = squares[0]
+    turned = mixed.T
+    a[:LANES, :LANES] = jnp.where(row <= col, mixed, turned)
+    a[:LANES, LANES:] = squares[1]
+    a[LANES:, :LANES] = jnp.zeros((LANES, LANES), jnp.float32)
+    a[LANES:, LANES:] = jnp.where(row > col, mixed, jnp.where(row < col, turned, chunks[0, 0, 4:5, :]))
 
 
 def reduce_kernel(sizes, rows_all, *refs):
@@ -119,10 +153,7 @@
     gram = local_gram(x_ref, freqs_ref, phases_ref, weight_ref, stored_ref, root_ref, feat, me, rows_all)
     feat_copy = pltpu.make_async_copy(feat, feat_out, feat_sem)
     feat_copy.start()
-    feats = gram.shape[0]
-    chunks = feats // 8
-    for side in range(2):
-        mine[side] = gram[:, side * LANES : (side + 1) * LANES].reshape(chunks, 8, LANES)
+    pack(gram, mine)
 
     pl.semaphore_wait(barrier, 1 + len(plane) + len(line))
 
@@ -223,9 +254,12 @@
         pivots = [None] * groups
         for k in range(block):
             gk, sk = divmod(k, 8)
-            pivot = spread(col[k], gk, sk)
+            pivot = spread(col[0], 0, 0) if k == 0 else coming
             pivots[gk] = pivot if sk == 0 else jnp.where(sub8 >= sk, pivot, pivots[gk])
             inv = 1.0 / pivot
+            if k + 1 < block:
+                gn, sn = divmod(k + 1, 8)
+                coming = spread(col[k + 1], gn, sn) - (spread(col[k], gn, sn) * spread(col[k + 1], gk, sk)) * inv
             mult = {}
             for g in range(gk, groups):
                 if g == gk and sk == 7:
@@ -276,9 +310,7 @@
     load = pltpu.make_async_copy(feat_in, feat, in_sem.at[1])
     load.start()
     first.wait()
-    feats = a.shape[0]
-    for side in range(2):
-        a[:, side * LANES : (side + 1) * LANES] = gram[side].reshape(feats, LANES)
+    unpack(gram, a)
     eliminate(a, factor, inverse, BLOCK)
     copies = [pltpu.make_async_copy(factor, factor_out, factor_sem)]
     copies[0].start()
@@ -327,11 +359,11 @@
     nx, nz, ny = sizes
     f32 = jnp.float32
     nplane, nline = nx * ny - 1, nz - 1
-    chunks = feats // 8
+    chunks = LANES // 4
     dma = pltpu.SemaphoreType.DMA
     gram, features = pl.pallas_call(
         functools.partial(reduce_kernel, sizes, rows_all),
-        out_shape=(jax.ShapeDtypeStruct((2, chunks, 8, LANES), f32), jax.ShapeDtypeStruct((rows, feats), f32)),
+        out_shape=(jax.ShapeDtypeStruct((2, chunks, CHUNK_ROWS, LANES), f32), jax.ShapeDtypeStruct((rows, feats), f32)),
         in_specs=[HBM()] * 6,
         out_specs=(HBM(), HBM()),
         scratch_shapes=[
@@ -343,12 +375,12 @@
             pltpu.SMEM(root.shape, jnp.int32),
             dma((6,)),
             pltpu.VMEM((rows, feats), f32),
-            pltpu.VMEM((2, chunks, 8, LANES), f32),
-            pltpu.VMEM((chunks, 8, LANES), f32),
-            pltpu.VMEM((chunks, 8, LANES), f32),
-            pltpu.VMEM((nplane, 8, LANES), f32),
-            pltpu.VMEM((nz, 8, LANES), f32),
-            pltpu.VMEM((chunks, 8, LANES), f32),
+            pltpu.VMEM((2, chunks, CHUNK_ROWS, LANES), f32),
+            pltpu.VMEM((chunks, CHUNK_ROWS, LANES), f32),
+            pltpu.VMEM((chunks, CHUNK_ROWS, LANES), f32),
+            pltpu.VMEM((nplane, CHUNK_ROWS, LANES), f32),
+            pltpu.VMEM((nz, CHUNK_ROWS, LANES), f32),
+            pltpu.VMEM((chunks, CHUNK_ROWS, LANES), f32),
             dma, dma, dma,
             dma((nplane,)), dma((nplane,)),
             dma((nline,)), dma((nline,)),
@@ -363,7 +395,7 @@
 
 def solution(mesh):
     groups, leaves = mesh.shape["grp"], mesh.shape["leaf"]
-    nx = 256 // 8 // leaves
+    nx = LANES // 4 // leaves
     sizes = (nx, groups // 2 // nx, leaves)
     return jax.shard_map(
         lambda inputs, *rest: per_device(sizes, inputs.shape[0] * groups * leaves, inputs, *rest),

time: 60.3 us -> 57.8 us (0.959)
  Pallas kernels: 59.5 us -> 57 us
    pallas_call x1, Pallas kernels: 48.3 us -> 46.3 us  [per_device(): pl.pallas_call(functools.partial(reduce_kernel, sizes, rows_all), out_sha...]
where the time goes in v3:
time: 57.8 us; the launch traced here: 57.6 us
  Pallas kernels  57 us (99%)
  between operations  0.64 us (1%)
    pallas_call x1, Pallas kernels, per_device(): pl.pallas_call(functools.partial(reduce_kernel, sizes, rows_all), out_sha...  46.3 us
    pallas_call x1, Pallas kernels, run_basis(): pl.pallas_call(basis_kernel, out_shape=(jax.ShapeDtypeStruct((feats, feat...  10.7 us

profile of v3, /device:TPU:1, one launch (start us, length us, event | category | flops | bytes accessed | tf_op | source)
XLA Modules:
  0.0 57.6 jit_solution(5818619892946174643)
XLA Ops:
  0.6 46.3 %reduce.1 = (f32[2,32,5,128]{3,2,1,0:T(8,128)}, f32[2048,256]{1,0:T(8,128)}) custom-call(f32[64,2048]{1,0:T(8,128)} %bitcast.3, f32[64,256]{1,0:T(8,128)} %refs_1_.1, f32[1,256]{1,0:T(1,128)} %bitcast.5, f32[16,128]{1,0:T(8,128)} %bitcast.4, f32[1,256,256]{2,1,0:T(8,128)} %refs_4_.1, s32[1024]{0:T(1024)} %refs_5_.1), custom_call_target="tpu_custom_call" | custom-call | tf_op jit(solution)/shard_map/reduce/pallas_call | solution.py:364
  46.9 10.7 %basis.1 = (f32[256,256]{1,0:T(8,128)}, f32[2048,256]{1,0:T(8,128)}) custom-call(f32[2,32,5,128]{3,2,1,0:T(8,128)} %get-tuple-element.4.gram_in, f32[2048,256]{1,0:T(8,128)} %get-tuple-element.5.feat_in), custom_call_target="tpu_custom_call" | custom-call | tf_op jit(solution)/shard_map/basis/pallas_call | solution.py:338

commit v4 on v3

--- a/solution.py
+++ b/solution.py
@@ -26,7 +26,7 @@
     nodes = top * (0.5 + 0.5 * np.cos((np.arange(64) + 0.5) * math.pi / 64))
     roots = np.sqrt(nodes)
     values = math.sqrt(2.0) * np.sin(roots / 2) / roots
-    fit = np.polynomial.chebyshev.Chebyshev.fit(nodes, values, 5, domain=[0, top])
+    fit = np.polynomial.chebyshev.Chebyshev.fit(nodes, values, 4, domain=[0, top])
     power = fit.convert(kind=np.polynomial.Polynomial)
     return [float(c) for c in power.coef]
 
@@ -120,8 +120,8 @@
 
 
 def reduce_loaded(sizes, rows_all, loads, x_ref, freqs_ref, phases_ref, weight_ref, stored_ref, root_ref,
-                  gram_out, feat_out, feat, mine, theirs, half, parts, zparts, back,
-                  feat_sem, core_send, core_recv, rs_send, rs_recv, z_send, z_recv, ag_send, ag_recv, end_send, end_recv, keep_sem):
+                  gram_out, feat_out, feat, mine, parts, zparts, done,
+                  feat_sem, keep_sem, rs_send, rs_recv, z_send, z_recv, ag_send, ag_recv):
     nx, nz, ny = sizes
     grp, leaf = lax.axis_index("grp"), lax.axis_index("leaf")
     core, z, x = lax.rem(grp, 2), lax.rem(grp // 2, nz), grp // (2 * nz)
@@ -129,21 +129,20 @@
     def at(x_, z_, core_, y_):
         return ((x_ * nz + z_) * 2 + core_, y_)
 
-    other = at(x, z, 1 - core, leaf)
     plane = []
     for dx in range(nx):
         for dy in range(ny):
-            if dx or dy:
-                plane.append((min(dx, nx - dx) + min(dy, ny - dy), dx, dy))
+            for dc in range(2):
+                if dx or dy or dc:
+                    plane.append((min(dx, nx - dx) + min(dy, ny - dy), dx, dy, dc))
     plane.sort(key=lambda t: -t[0])
-    plane = [(lax.rem(x + dx, nx), lax.rem(leaf + dy, ny)) for _, dx, dy in plane]
+    plane = [(lax.rem(x + dx, nx), lax.rem(leaf + dy, ny), lax.rem(core + dc, 2)) for _, dx, dy, dc in plane]
     line = sorted(range(1, nz), key=lambda d: -min(d, nz - d))
     line = [lax.rem(z + dz, nz) for dz in line]
 
     barrier = pltpu.get_barrier_semaphore()
-    pl.semaphore_signal(barrier, inc=1, device_id=other, device_id_type=MESH)
-    for px, py in plane:
-        pl.semaphore_signal(barrier, inc=1, device_id=at(px, z, core, py), device_id_type=MESH)
+    for px, py, pc in plane:
+        pl.semaphore_signal(barrier, inc=1, device_id=at(px, z, pc, py), device_id_type=MESH)
     for pz in line:
         pl.semaphore_signal(barrier, inc=1, device_id=at(x, pz, core, leaf), device_id_type=MESH)
 
@@ -155,23 +154,17 @@
     feat_copy.start()
     pack(gram, mine)
 
-    pl.semaphore_wait(barrier, 1 + len(plane) + len(line))
-
-    swap = pltpu.make_async_remote_copy(mine.at[1 - core], theirs, core_send, core_recv, device_id=other, device_id_type=MESH)
-    swap.start()
-    swap.wait_recv()
-    half[...] = mine[core] + theirs[...]
+    pl.semaphore_wait(barrier, len(plane) + len(line))
 
     spot = x * ny + leaf
     copies = []
-    for n, (px, py) in enumerate(plane):
-        there = px * ny + py
+    for n, (px, py, pc) in enumerate(plane):
         copies.append(pltpu.make_async_remote_copy(
-            half.at[there], parts.at[n], rs_send.at[n], rs_recv.at[n],
-            device_id=at(px, z, core, py), device_id_type=MESH))
+            mine.at[pc, px * ny + py], parts.at[n], rs_send.at[n], rs_recv.at[n],
+            device_id=at(px, z, pc, py), device_id_type=MESH))
     for c in copies:
         c.start()
-    total = half[spot]
+    total = mine[core, spot]
     for n in reversed(range(len(copies))):
         copies[n].wait_recv()
         total = total + parts[n]
@@ -190,26 +183,22 @@
     for k in range(1, nz):
         total = total + zparts[k]
 
-    back[spot] = total
+    done[...] = total
     spread = []
-    for n, (px, py) in enumerate(plane):
+    for n, (px, py, pc) in enumerate(plane):
         spread.append(pltpu.make_async_remote_copy(
-            back.at[spot], back.at[spot], ag_send.at[n], ag_recv.at[n],
-            device_id=at(px, z, core, py), device_id_type=MESH))
+            done, gram_out.at[core, spot], ag_send.at[n], ag_recv.at[n],
+            device_id=at(px, z, pc, py), device_id_type=MESH))
     for c in spread:
         c.start()
-    for c in spread:
-        c.wait_recv()
-
-    end = pltpu.make_async_remote_copy(back, gram_out.at[core], end_send, end_recv, device_id=other, device_id_type=MESH)
-    end.start()
-    keep = pltpu.make_async_copy(back, gram_out.at[core], keep_sem)
+    keep = pltpu.make_async_copy(done, gram_out.at[core, spot], keep_sem)
     keep.start()
-    for c in [swap] + copies + lines + spread:
+    for c in copies + lines + spread:
         c.wait_send()
     feat_copy.wait()
     keep.wait()
-    end.wait()
+    for c in spread:
+        c.wait_recv()
 
 
 def columns(values, first, block):
@@ -294,8 +283,11 @@
             a[r1:, :] = jnp.where(within(cols_rest, r0 - block), 0.0, a[r1:, :]) - drop
         if r2 < n:
             both = jnp.where(cols_of >= r1, full, lower)
-            left = upper.T[r2:, :]
-            drop = lax.dot_general(left, both, (((1,), (0,)), ((), ())), precision=HIGHEST, preferred_element_type=jnp.float32)
+            high, middle, low = pieces(upper)
+            left = jnp.concatenate([high, high, middle, middle, high, low], axis=0).T[r2:, :]
+            high, middle, low = pieces(both)
+            right = jnp.concatenate([high, middle, high, middle, low, high], axis=0)
+            drop = jnp.dot(left, right, preferred_element_type=jnp.float32)
         if ahead:
             taken = [jnp.concatenate(part, axis=0) for part in gone]
             rest = jnp.concatenate(taken[:ntile], axis=1)
@@ -358,7 +350,7 @@
     rows, feats = inputs.shape[0], freqs.shape[1]
     nx, nz, ny = sizes
     f32 = jnp.float32
-    nplane, nline = nx * ny - 1, nz - 1
+    nplane, nline = 2 * nx * ny - 1, nz - 1
     chunks = LANES // 4
     dma = pltpu.SemaphoreType.DMA
     gram, features = pl.pallas_call(
@@ -376,16 +368,13 @@
             dma((6,)),
             pltpu.VMEM((rows, feats), f32),
             pltpu.VMEM((2, chunks, CHUNK_ROWS, LANES), f32),
-            pltpu.VMEM((chunks, CHUNK_ROWS, LANES), f32),
-            pltpu.VMEM((chunks, CHUNK_ROWS, LANES), f32),
             pltpu.VMEM((nplane, CHUNK_ROWS, LANES), f32),
             pltpu.VMEM((nz, CHUNK_ROWS, LANES), f32),
-            pltpu.VMEM((chunks, CHUNK_ROWS, LANES), f32),
-            dma, dma, dma,
+            pltpu.VMEM((CHUNK_ROWS, LANES), f32),
+            dma, dma,
             dma((nplane,)), dma((nplane,)),
             dma((nline,)), dma((nline,)),
             dma((nplane,)), dma((nplane,)),
-            dma, dma, dma,
         ],
         compiler_params=pltpu.CompilerParams(collective_id=0, has_side_effects=True, vmem_limit_bytes=60 * 2**20),
         name="reduce",

time: 57.8 us -> 58.5 us (1.012)
  Pallas kernels: 57 us -> 57.7 us
    pallas_call x1, Pallas kernels: 46.3 us -> 47.9 us  [per_device(): pl.pallas_call(functools.partial(reduce_kernel, sizes, rows_all), out_sha...]
    pallas_call x1, Pallas kernels: 10.7 us -> 9.76 us  [run_basis(): pl.pallas_call(basis_kernel, out_shape=(jax.ShapeDtypeStruct((feats, feat...]
where the time goes in v4:
time: 58.5 us; the launch traced here: 58.3 us
  Pallas kernels  57.7 us (99%)
  between operations  0.64 us (1%)
    pallas_call x1, Pallas kernels, per_device(): pl.pallas_call(functools.partial(reduce_kernel, sizes, rows_all), out_sha...  47.9 us
    pallas_call x1, Pallas kernels, run_basis(): pl.pallas_call(basis_kernel, out_shape=(jax.ShapeDtypeStruct((feats, feat...  9.76 us

profile of v4, /device:TPU:1, one launch (start us, length us, event | category | flops | bytes accessed | tf_op | source)
XLA Modules:
  0.0 58.3 jit_solution(6415635531637438398)
XLA Ops:
  0.6 47.9 %reduce.1 = (f32[2,32,5,128]{3,2,1,0:T(8,128)}, f32[2048,256]{1,0:T(8,128)}) custom-call(f32[64,2048]{1,0:T(8,128)} %bitcast.3, f32[64,256]{1,0:T(8,128)} %refs_1_.1, f32[1,256]{1,0:T(1,128)} %bitcast.5, f32[16,128]{1,0:T(8,128)} %bitcast.4, f32[1,256,256]{2,1,0:T(8,128)} %refs_4_.1, s32[1024]{0:T(1024)} %refs_5_.1), custom_call_target="tpu_custom_call" | custom-call | tf_op jit(solution)/shard_map/reduce/pallas_call | solution.py:356
  48.6 9.8 %basis.1 = (f32[256,256]{1,0:T(8,128)}, f32[2048,256]{1,0:T(8,128)}) custom-call(f32[2,32,5,128]{3,2,1,0:T(8,128)} %get-tuple-element.4.gram_in, f32[2048,256]{1,0:T(8,128)} %get-tuple-element.5.feat_in), custom_call_target="tpu_custom_call" | custom-call | tf_op jit(solution)/shard_map/basis/pallas_call | solution.py:330

commit v5 on v3

--- a/solution.py
+++ b/solution.py
@@ -26,7 +26,7 @@
     nodes = top * (0.5 + 0.5 * np.cos((np.arange(64) + 0.5) * math.pi / 64))
     roots = np.sqrt(nodes)
     values = math.sqrt(2.0) * np.sin(roots / 2) / roots
-    fit = np.polynomial.chebyshev.Chebyshev.fit(nodes, values, 5, domain=[0, top])
+    fit = np.polynomial.chebyshev.Chebyshev.fit(nodes, values, 4, domain=[0, top])
     power = fit.convert(kind=np.polynomial.Polynomial)
     return [float(c) for c in power.coef]
 
@@ -294,8 +294,11 @@
             a[r1:, :] = jnp.where(within(cols_rest, r0 - block), 0.0, a[r1:, :]) - drop
         if r2 < n:
             both = jnp.where(cols_of >= r1, full, lower)
-            left = upper.T[r2:, :]
-            drop = lax.dot_general(left, both, (((1,), (0,)), ((), ())), precision=HIGHEST, preferred_element_type=jnp.float32)
+            high, middle, low = pieces(upper)
+            left = jnp.concatenate([high, high, middle, middle, high, low], axis=0).T[r2:, :]
+            high, middle, low = pieces(both)
+            right = jnp.concatenate([high, middle, high, middle, low, high], axis=0)
+            drop = jnp.dot(left, right, preferred_element_type=jnp.float32)
         if ahead:
             taken = [jnp.concatenate(part, axis=0) for part in gone]
             rest = jnp.concatenate(taken[:ntile], axis=1)

time: 57.8 us -> 56.8 us (0.983)
  Pallas kernels: 57 us -> 56 us
    pallas_call x1, Pallas kernels: 10.7 us -> 9.75 us  [run_basis(): pl.pallas_call(basis_kernel, out_shape=(jax.ShapeDtypeStruct((feats, feat...]
where the time goes in v5:
time: 56.8 us; the launch traced here: 56.6 us
  Pallas kernels  56 us (99%)
  between operations  0.64 us (1%)
    pallas_call x1, Pallas kernels, per_device(): pl.pallas_call(functools.partial(reduce_kernel, sizes, rows_all), out_sha...  46.3 us
    pallas_call x1, Pallas kernels, run_basis(): pl.pallas_call(basis_kernel, out_shape=(jax.ShapeDtypeStruct((feats, feat...  9.75 us

profile of v5, /device:TPU:1, one launch (start us, length us, event | category | flops | bytes accessed | tf_op | source)
XLA Modules:
  0.0 56.6 jit_solution(5728374929941417174)
XLA Ops:
  0.6 46.3 %reduce.1 = (f32[2,32,5,128]{3,2,1,0:T(8,128)}, f32[2048,256]{1,0:T(8,128)}) custom-call(f32[64,2048]{1,0:T(8,128)} %bitcast.3, f32[64,256]{1,0:T(8,128)} %refs_1_.1, f32[1,256]{1,0:T(1,128)} %bitcast.5, f32[16,128]{1,0:T(8,128)} %bitcast.4, f32[1,256,256]{2,1,0:T(8,128)} %refs_4_.1, s32[1024]{0:T(1024)} %refs_5_.1), custom_call_target="tpu_custom_call" | custom-call | tf_op jit(solution)/shard_map/reduce/pallas_call | solution.py:367
  46.9 9.8 %basis.1 = (f32[256,256]{1,0:T(8,128)}, f32[2048,256]{1,0:T(8,128)}) custom-call(f32[2,32,5,128]{3,2,1,0:T(8,128)} %get-tuple-element.4.gram_in, f32[2048,256]{1,0:T(8,128)} %get-tuple-element.5.feat_in), custom_call_target="tpu_custom_call" | custom-call | tf_op jit(solution)/shard_map/basis/pallas_call | solution.py:341
